TPU v7x, 32 devices: a whole 2x2x4 slice. The times are simulated.
32 devices in a mesh: dp: 8 (over y, x, core), seq: 4 (over z).
Axes of the slice: x: 2, y: 2, z: 4, core: 2. Of those that a mesh axis runs over, the one named last changes fastest.
Arguments:
- tokens: bfloat16 [16, 1024, 512], P('dp', 'seq'), may hold values from -6 to 6
- memory: bfloat16 [16, 1024, 512], P('dp', 'seq'), may hold values from -6 to 6
- tgt_segments: int32 [16, 1024], P('dp'), may hold values from 0 to 2, as said below
- mem_segments: int32 [16, 1024], P('dp'), may hold values from 0 to 2, as said below
- cotangent: bfloat16 [16, 1024, 512], P('dp', 'seq'), may hold values from -6 to 6
- w_qkv: bfloat16 [512, 1536], replicated, may hold values from -0.25 to 0.25
- w_self_out: bfloat16 [512, 512], replicated, may hold values from -1.5 to 1.5
- w_cross_q: bfloat16 [512, 512], replicated, may hold values from -0.25 to 0.25
- w_cross_kv: bfloat16 [512, 1024], replicated, may hold values from -0.25 to 0.25
- w_cross_out: bfloat16 [512, 512], replicated, may hold values from -1.5 to 1.5
- w_up: bfloat16 [512, 2048], replicated, may hold values from -0.25 to 0.25
- w_down: bfloat16 [2048, 512], replicated, may hold values from -0.125 to 0.125
- ln1_gain: float32 [512], replicated, may hold values from 0.25 to 1.75
- ln1_bias: float32 [512], replicated, may hold values from -1.8 to 1.8
- ln2_gain: float32 [512], replicated, may hold values from 0.25 to 1.75
- ln2_bias: float32 [512], replicated, may hold values from -1.8 to 1.8
- ln3_gain: float32 [512], replicated, may hold values from 0.25 to 1.75
- ln3_bias: float32 [512], replicated, may hold values from -1.8 to 1.8
Outputs:
- output: bfloat16 [16, 1024, 512], P('dp', 'seq')
- grad_tokens: float32 [16, 1024, 512], P('dp', 'seq')
- grad_memory: float32 [16, 1024, 512], P('dp', 'seq')
- grad_w_qkv: float32 [512, 1536], replicated
- grad_w_self_out: float32 [512, 512], replicated
- grad_w_cross_q: float32 [512, 512], replicated
- grad_w_cross_kv: float32 [512, 1024], replicated
- grad_w_cross_out: float32 [512, 512], replicated
- grad_w_up: float32 [512, 2048], replicated
- grad_w_down: float32 [2048, 512], replicated
- grad_ln1_gain: float32 [512], replicated
- grad_ln1_bias: float32 [512], replicated
- grad_ln2_gain: float32 [512], replicated
- grad_ln2_bias: float32 [512], replicated
- grad_ln3_gain: float32 [512], replicated
- grad_ln3_bias: float32 [512], replicated
Inputs may be any that keep to these rules, and one draw needn't show every extreme that they name: `tgt_segments`: along a row the ids never fall and all three occur; document 1 begins within the row's first 256 positions and ends within its last 256. `mem_segments`: along a row the ids never fall and all three occur.
All inputs are finite; a program needn't handle non-finite values.
Results may differ from a plain program's by a relative error of at most 0.02.
Values may be sent and summed in bfloat16 or wider, within the bound.
No kernel may reach another device: no remote copies, remote signals or barrier semaphores. Data moves between devices by JAX's collectives and lax.ppermute only.
A program may use at most 128 MiB of HBM per device.

v0:
```python
import math
import jax
import jax.numpy as jnp
from jax import lax
from jax.sharding import PartitionSpec as P

HEAD_DIM = 64


def mat_dot(left, right):
    return jnp.dot(left, right, preferred_element_type=jnp.float32)


def left_dot(left, right):
    return lax.dot_general(
        left, right, (((0,), (0,)), ((), ())), preferred_element_type=jnp.float32
    )


def right_dot(left, right):
    return lax.dot_general(
        left, right, (((1,), (1,)), ((), ())), preferred_element_type=jnp.float32
    )


def layer_norm(values, gain, bias):
    centre = values - jnp.mean(values, axis=-1, keepdims=True)
    recip = lax.rsqrt(jnp.mean(centre * centre, axis=-1, keepdims=True) + 1e-05)
    normed = centre * recip
    return (normed * gain + bias, normed, recip)


def norm_back(grad_out, normed, recip, gain):
    grad_gain = jnp.sum(grad_out * normed, axis=0)
    grad_bias = jnp.sum(grad_out, axis=0)
    scaled = grad_out * gain
    grad_in = recip * (
        scaled
        - jnp.mean(scaled, axis=-1, keepdims=True)
        - normed * jnp.mean(scaled * normed, axis=-1, keepdims=True)
    )
    return (grad_in, grad_gain, grad_bias)


def causal_mask(segment_row):
    place = jnp.arange(segment_row.shape[0])
    return (place[None, :] <= place[:, None]) & (segment_row[:, None] == segment_row[None, :])


def cross_mask(tgt_row, mem_row):
    return tgt_row[:, None] == mem_row[None, :]


def masked_scores(queries, key_heads, allowed, score_scale):
    scores = (
        jnp.einsum("qhd,khd->hqk", queries, key_heads, preferred_element_type=jnp.float32)
        * score_scale
    )
    return jnp.where(allowed[None], scores, -1000000000.0)


def attend_forward(queries, key_heads, value_heads, allowed, score_scale):
    scores = masked_scores(queries, key_heads, allowed, score_scale)
    highest = jnp.max(scores, axis=-1, keepdims=True)
    expo = jnp.exp(scores - highest)
    total = jnp.sum(expo, axis=-1, keepdims=True)
    probs = (expo / total).astype(jnp.bfloat16)
    context = jnp.einsum("hqk,khd->qhd", probs, value_heads, preferred_element_type=jnp.float32)
    return (context.astype(jnp.bfloat16), highest + jnp.log(total))


def attend_backward(queries, key_heads, value_heads, log_total, d_context, allowed, score_scale):
    scores = masked_scores(queries, key_heads, allowed, score_scale)
    probs = jnp.exp(scores - log_total)
    d_values = jnp.einsum(
        "hqk,qhd->khd", probs.astype(jnp.bfloat16), d_context, preferred_element_type=jnp.float32
    ).astype(jnp.bfloat16)
    d_probs = jnp.einsum("qhd,khd->hqk", d_context, value_heads, preferred_element_type=jnp.float32)
    centre = jnp.sum(probs * d_probs, axis=-1, keepdims=True)
    d_scores = (probs * (d_probs - centre)).astype(jnp.bfloat16)
    d_queries = (
        jnp.einsum("hqk,khd->qhd", d_scores, key_heads, preferred_element_type=jnp.float32)
        * score_scale
    ).astype(jnp.bfloat16)
    d_keys = (
        jnp.einsum("hqk,qhd->khd", d_scores, queries, preferred_element_type=jnp.float32)
        * score_scale
    ).astype(jnp.bfloat16)
    return (d_queries, d_keys, d_values)


def body(
    tokens,
    memory,
    tgt_segments,
    mem_segments,
    cotangent,
    w_qkv,
    w_self_out,
    w_cross_q,
    w_cross_kv,
    w_cross_out,
    w_up,
    w_down,
    ln1_gain,
    ln1_bias,
    ln2_gain,
    ln2_bias,
    ln3_gain,
    ln3_bias,
):
    row_count, tok_local, model_width = tokens.shape
    mem_local = memory.shape[1]
    seq_parts = lax.axis_size("seq")
    head_share = model_width // seq_parts
    heads_here = head_share // HEAD_DIM
    seq_len = tgt_segments.shape[1]
    mem_len = mem_segments.shape[1]
    score_scale = 1.0 / math.sqrt(HEAD_DIM)
    token_total = row_count * tok_local
    flat_tokens = tokens.reshape(token_total, model_width)
    flat_memory = memory.reshape(row_count * mem_local, model_width)
    mixed_proj = (
        mat_dot(flat_tokens, w_qkv)
        .astype(jnp.bfloat16)
        .reshape(row_count, tok_local, 3, seq_parts, head_share)
    )
    self_heads = lax.all_to_all(mixed_proj, "seq", split_axis=3, concat_axis=1, tiled=True).reshape(
        row_count, seq_len, 3, heads_here, HEAD_DIM
    )
    memory_proj = (
        mat_dot(flat_memory, w_cross_kv)
        .astype(jnp.bfloat16)
        .reshape(row_count, mem_local, 2, seq_parts, head_share)
    )
    memory_heads = lax.all_to_all(
        memory_proj, "seq", split_axis=3, concat_axis=1, tiled=True
    ).reshape(row_count, mem_len, 2, heads_here, HEAD_DIM)
    self_q = self_heads[:, :, 0]
    self_k = self_heads[:, :, 1]
    self_v = self_heads[:, :, 2]
    memory_k = memory_heads[:, :, 0]
    memory_v = memory_heads[:, :, 1]

    def self_forward(row_item):
        queries, key_heads, value_heads, segment_row = row_item
        return attend_forward(
            queries, key_heads, value_heads, causal_mask(segment_row), score_scale
        )

    self_context, self_lse = lax.map(self_forward, (self_q, self_k, self_v, tgt_segments))
    self_back = lax.all_to_all(
        self_context.reshape(row_count, seq_len, 1, head_share),
        "seq",
        split_axis=1,
        concat_axis=2,
        tiled=True,
    )
    context_one = self_back.reshape(token_total, model_width)
    attn_one = mat_dot(context_one, w_self_out)
    norm_one, normed_one, recip_one = layer_norm(
        flat_tokens.astype(jnp.float32) + attn_one, ln1_gain, ln1_bias
    )
    norm_one_low = norm_one.astype(jnp.bfloat16)
    cross_proj = (
        mat_dot(norm_one_low, w_cross_q)
        .astype(jnp.bfloat16)
        .reshape(row_count, tok_local, 1, seq_parts, head_share)
    )
    cross_q = lax.all_to_all(cross_proj, "seq", split_axis=3, concat_axis=1, tiled=True).reshape(
        row_count, seq_len, heads_here, HEAD_DIM
    )

    def cross_forward(row_item):
        queries, key_heads, value_heads, tgt_row, mem_row = row_item
        return attend_forward(
            queries, key_heads, value_heads, cross_mask(tgt_row, mem_row), score_scale
        )

    cross_context, cross_lse = lax.map(
        cross_forward, (cross_q, memory_k, memory_v, tgt_segments, mem_segments)
    )
    cross_back = lax.all_to_all(
        cross_context.reshape(row_count, seq_len, 1, head_share),
        "seq",
        split_axis=1,
        concat_axis=2,
        tiled=True,
    )
    context_two = cross_back.reshape(token_total, model_width)
    attn_two = mat_dot(context_two, w_cross_out)
    norm_two, normed_two, recip_two = layer_norm(norm_one + attn_two, ln2_gain, ln2_bias)
    norm_two_low = norm_two.astype(jnp.bfloat16)
    pre_act = mat_dot(norm_two_low, w_up)
    sigma = jax.nn.sigmoid(pre_act)
    hidden_low = (pre_act * sigma).astype(jnp.bfloat16)
    fed = mat_dot(hidden_low, w_down)
    result, normed_three, recip_three = layer_norm(norm_two + fed, ln3_gain, ln3_bias)
    output = result.astype(jnp.bfloat16).reshape(row_count, tok_local, model_width)
    grad_out = cotangent.reshape(token_total, model_width).astype(jnp.float32)
    d_resid_three, d_gain_three, d_bias_three = norm_back(
        grad_out, normed_three, recip_three, ln3_gain
    )
    d_fed_low = d_resid_three.astype(jnp.bfloat16)
    grad_down = left_dot(hidden_low, d_fed_low)
    d_hidden = right_dot(d_fed_low, w_down)
    d_pre_low = (d_hidden * sigma * (1.0 + pre_act * (1.0 - sigma))).astype(jnp.bfloat16)
    grad_up = left_dot(norm_two_low, d_pre_low)
    d_norm_two = d_resid_three + right_dot(d_pre_low, w_up)
    d_resid_two, d_gain_two, d_bias_two = norm_back(d_norm_two, normed_two, recip_two, ln2_gain)
    d_attn_two = d_resid_two.astype(jnp.bfloat16)
    grad_cross_out = left_dot(context_two, d_attn_two)
    d_context_two = (
        right_dot(d_attn_two, w_cross_out)
        .astype(jnp.bfloat16)
        .reshape(row_count, tok_local, seq_parts, head_share)
    )
    d_cross_heads = lax.all_to_all(
        d_context_two, "seq", split_axis=2, concat_axis=1, tiled=True
    ).reshape(row_count, seq_len, heads_here, HEAD_DIM)

    def cross_backward(row_item):
        queries, key_heads, value_heads, log_total, d_context, tgt_row, mem_row = row_item
        return attend_backward(
            queries,
            key_heads,
            value_heads,
            log_total,
            d_context,
            cross_mask(tgt_row, mem_row),
            score_scale,
        )

    d_cross_q, d_mem_keys, d_mem_values = lax.map(
        cross_backward,
        (cross_q, memory_k, memory_v, cross_lse, d_cross_heads, tgt_segments, mem_segments),
    )
    d_memory_kv = jnp.stack((d_mem_keys, d_mem_values), axis=2).reshape(
        row_count, mem_len, 2, 1, head_share
    )
    back_query, back_memory = (
        lax.all_to_all(
            d_cross_q.reshape(row_count, seq_len, 1, 1, head_share),
            "seq",
            split_axis=1,
            concat_axis=3,
            tiled=True,
        ),
        lax.all_to_all(d_memory_kv, "seq", split_axis=1, concat_axis=3, tiled=True),
    )
    d_query_flat = back_query.reshape(token_total, model_width)
    d_memory_flat = back_memory.reshape(row_count * mem_local, 2 * model_width)
    grad_cross_q = left_dot(norm_one_low, d_query_flat)
    grad_cross_kv = left_dot(flat_memory, d_memory_flat)
    grad_memory = right_dot(d_memory_flat, w_cross_kv).reshape(row_count, mem_local, model_width)
    d_norm_one = d_resid_two + right_dot(d_query_flat, w_cross_q)
    d_resid_one, d_gain_one, d_bias_one = norm_back(d_norm_one, normed_one, recip_one, ln1_gain)
    d_attn_one = d_resid_one.astype(jnp.bfloat16)
    grad_self_out = left_dot(context_one, d_attn_one)
    d_context_one = (
        right_dot(d_attn_one, w_self_out)
        .astype(jnp.bfloat16)
        .reshape(row_count, tok_local, seq_parts, head_share)
    )
    d_self_heads = lax.all_to_all(
        d_context_one, "seq", split_axis=2, concat_axis=1, tiled=True
    ).reshape(row_count, seq_len, heads_here, HEAD_DIM)

    def self_backward(row_item):
        queries, key_heads, value_heads, log_total, d_context, segment_row = row_item
        return attend_backward(
            queries,
            key_heads,
            value_heads,
            log_total,
            d_context,
            causal_mask(segment_row),
            score_scale,
        )

    d_self_q, d_self_k, d_self_v = lax.map(
        self_backward, (self_q, self_k, self_v, self_lse, d_self_heads, tgt_segments)
    )
    d_mixed = jnp.stack((d_self_q, d_self_k, d_self_v), axis=2).reshape(
        row_count, seq_len, 3, 1, head_share
    )
    back_mixed = lax.all_to_all(d_mixed, "seq", split_axis=1, concat_axis=3, tiled=True).reshape(
        token_total, 3 * model_width
    )
    grad_qkv = left_dot(flat_tokens, back_mixed)
    grad_tokens = (d_resid_one + right_dot(back_mixed, w_qkv)).reshape(
        row_count, tok_local, model_width
    )
    summed = lax.psum(
        (
            grad_qkv,
            grad_self_out,
            grad_cross_q,
            grad_cross_kv,
            grad_cross_out,
            grad_up,
            grad_down,
            d_gain_one,
            d_bias_one,
            d_gain_two,
            d_bias_two,
            d_gain_three,
            d_bias_three,
        ),
        ("dp", "seq"),
    )
    return (
        output,
        grad_tokens,
        grad_memory,
        summed[0],
        summed[1],
        summed[2],
        summed[3],
        summed[4],
        summed[5],
        summed[6],
        summed[7],
        summed[8],
        summed[9],
        summed[10],
        summed[11],
        summed[12],
    )


def solution(mesh):
    return jax.shard_map(
        body,
        mesh=mesh,
        in_specs=(
            P("dp", "seq", None),
            P("dp", "seq", None),
            P("dp", None),
            P("dp", None),
            P("dp", "seq", None),
            P(),
            P(),
            P(),
            P(),
            P(),
            P(),
            P(),
            P(),
            P(),
            P(),
            P(),
            P(),
            P(),
        ),
        out_specs=(
            P("dp", "seq", None),
            P("dp", "seq", None),
            P("dp", "seq", None),
            P(),
            P(),
            P(),
            P(),
            P(),
            P(),
            P(),
            P(),
            P(),
            P(),
            P(),
            P(),
            P(),
        ),
        check_vma=False,
    )
```

profile of v0, /device:TPU:0, one launch (start us, length us, event | category | flops | bytes accessed | tf_op | source)
XLA Modules:
  0.0 717.0 jit_solution(7663693203559814328)
XLA Ops:
  7.2 3.8 convolution_convert_fusion
  11.0 3.9 reshape.401
  15.0 2.9 copy.196
  17.9 6.3 all-to-all-start
  24.2 37.1 %all-to-all-done = bf16[2,256,3,4,128]{4,1,2,0,3:T(8,128)(2,1)} async-done(((bf16[2,256,3,4,128]{4,1,2,0,3:T(8,128)(2,1)}), bf16[2,256,3,4,128]{4,1,2,0,3:T(8,128)(2,1)}, u32[]{:S(2)}, u32[]{:S(2)}) %all-to-all-start) | async-done | bytes 1572896 | tf_op jit(solution)/shard_map/all_to_all | solution.py:128
  61.3 3.8 copy.197
  65.0 3.8 reshape.402
  72.0 16.4 %while.52 = (s32[]{:T(128)}, bf16[2,1024,2,64]{1,3,2,0:T(8,128)(2,1)}, f32[2,2,1024,1]{2,1,3,0:T(2,128)S(1)}, bf16[2,1024,2,64]{1,3,2,0:T(8,128)(2,1)}, s32[2,10...) while((s32[]{:T(128)}, ...), condition=%wide.region_3.4_spmd, body=%wide.region_0.3_spmd.sunk | while | flops 565311488 | bytes 36780216 | solution.py:151
  76.6 2.8 fusion.227
  84.8 2.8 fusion.227
  90.7 4.1 all-to-all-start.1
  94.8 3.1 convolution_convert_fusion.1
  97.9 2.6 reshape.406
  100.5 3.0 copy.201
  103.5 5.4 all-to-all-done.1
  108.9 4.3 all-to-all-start.2
  122.7 15.7 %all-to-all-done.2 = bf16[2,256,2,4,128]{4,2,1,0,3:T(2,128)(2,1)} async-done(((bf16[2,256,2,4,128]{4,2,1,0,3:T(2,128)(2,1)}), bf16[2,256,2,4,128]{4,2,1,0,3:T(2,128)(2,1)}, u32[]{:S(2)}, u32[]{:S(2)}) %all-to-all-start.2) | async-done | bytes 1048608 | tf_op jit(solution)/shard_map/all_to_all | solution.py:136
  138.4 4.4 all-to-all-start.3
  142.9 3.8 copy.202
  146.7 2.6 reshape.407
  151.5 5.4 all-to-all-done.3
  162.1 18.5 %while.53 = (s32[]{:T(128)}, bf16[2,1024,2,64]{1,3,2,0:T(8,128)(2,1)}, f32[2,2,1024,1]{2,1,3,0:T(2,128)S(1)}, bf16[2,1024,2,64]{1,3,2,0:T(8,128)(2,1)}, s32[2,10...) while((s32[]{:T(128)}, ...), condition=%wide.region_9.10_spmd, body=%wide.region_6.9_spmd.sunk | while | flops 563214336 | bytes 36792512 | solution.py:180
  162.8 2.9 fusion.229
  167.7 2.8 fusion.231
  172.0 2.9 fusion.229
  177.0 2.8 fusion.231
  182.6 4.8 all-to-all-start.4
  189.4 12.1 %all-to-all-done.4 = bf16[2,1024,1,128]{3,0,2,1:T(2,128)(2,1)} async-done(((bf16[2,1024,1,128]{3,0,2,1:T(2,128)(2,1)}), bf16[2,1024,1,128]{3,0,2,1:T(2,128)(2,1)}, u32[]{:S(2)}, u32[]{:S(2)}) %all-to-all-start.4) | async-done | bytes 524320 | tf_op jit(solution)/shard_map/all_to_all | solution.py:183
  221.2 4.3 all-to-all-start.5
  225.5 14.1 %all-to-all-done.5 = bf16[2,256,4,128]{3,1,0,2:T(8,128)(2,1)} async-done(((bf16[2,256,4,128]{3,1,0,2:T(8,128)(2,1)}), bf16[2,256,4,128]{3,1,0,2:T(8,128)(2,1)}, u32[]{:S(2)}, u32[]{:S(2)}) %all-to-all-start.5) | async-done | bytes 524320 | tf_op jit(solution)/shard_map/all_to_all | solution.py:218
  246.6 27.1 %while.54 = (s32[]{:T(128)}, bf16[2,1024,2,64]{1,3,2,0:T(8,128)(2,1)}, bf16[2,1024,2,64]{1,3,2,0:T(8,128)(2,1)}, bf16[2,1024,2,64]{1,3,2,0:T(8,128)(2,1)}, bf16[...) while((s32[]{:T(128)}, ...), condition=%wide.region_20.21_spmd, body=%wide.region_18.20_spmd.sunk | while | flops 1375336448 | bytes 86594928 | solution.py:234
  248.6 3.0 multiply_reduce_fusion.13
  251.6 2.7 multiply_convert_fusion.8
  256.8 2.5 fusion.243
  262.2 3.0 multiply_reduce_fusion.13
  265.2 2.7 multiply_convert_fusion.8
  270.4 2.5 fusion.243
  275.1 16.4 %all_to_all.150 = bf16[2,1024,1,1,128]{4,0,3,2,1:T(2,128)(2,1)S(1)} all-to-all(bf16[2,1024,1,1,128]{4,0,3,2,1:T(2,128)(2,1)S(1)} %copy.210), channel_id=1, replica_groups=mesh['dp'=8,'seq'=4] {'seq'}, dimensions={1} | all-to-all | bytes 1048576 | tf_op jit(solution)/shard_map/all_to_all | solution.py:242
  296.0 4.1 all-to-all-start.7
  303.5 10.2 %all-to-all-done.7 = bf16[2,256,4,128]{3,1,0,2:T(8,128)(2,1)} async-done(((bf16[2,256,4,128]{3,1,0,2:T(8,128)(2,1)}), bf16[2,256,4,128]{3,1,0,2:T(8,128)(2,1)}, u32[]{:S(2)}, u32[]{:S(2)}) %all-to-all-start.7) | async-done | bytes 524320 | tf_op jit(solution)/shard_map/all_to_all | solution.py:265
  313.7 4.5 all-to-all-start.9
  323.4 27.0 %while.55 = (s32[]{:T(128)}, bf16[2,1024,2,64]{1,3,2,0:T(8,128)(2,1)}, bf16[2,1024,2,64]{1,3,2,0:T(8,128)(2,1)}, bf16[2,1024,2,64]{1,3,2,0:T(8,128)(2,1)}, bf16[...) while((s32[]{:T(128)}, ...), condition=%wide.region_25.26_spmd, body=%wide.region_23.25_spmd.sunk | while | flops 1377433600 | bytes 86582632 | solution.py:281
  325.4 3.0 multiply_reduce_fusion.14
  328.4 2.7 multiply_convert_fusion.9
  333.5 2.5 fusion.256
  338.9 3.0 multiply_reduce_fusion.14
  341.9 2.7 multiply_convert_fusion.9
  347.0 2.5 fusion.256
  350.4 2.8 pad_maximum_fusion
  353.2 5.0 copy.215
  358.2 5.1 all-to-all-start.8
  363.7 2.5 fusion.134
  366.2 5.2 fusion.153
  371.4 3.5 fusion.150
  383.1 16.2 %all-to-all-done.8 = bf16[2,1024,3,1,128]{4,0,3,2,1:T(2,128)(2,1)} async-done(((bf16[2,1024,3,1,128]{4,0,3,2,1:T(2,128)(2,1)}), bf16[2,1024,3,1,128]{4,0,3,2,1:T(2,128)(2,1)}, u32[]{:S(2)}, u32[]{:S(2)}) %all-to-all-start.8) | async-done | bytes 1572896 | tf_op jit(solution)/shard_map/all_to_all | solution.py:287
  400.9 2.4 copy.217
  403.3 2.8 reshape.419
  406.1 2.7 convolution_bitcast_fusion
  409.5 40.1 %all-reduce = (f32[512]{0:T(512)}, f32[512]{0:T(512)}, f32[512]{0:T(512)}, f32[512]{0:T(512)}, f32[512]{0:T(512)}, /*index=5*/f32[512]{0:T(512)}) all-reduce(f32[512]{0:T(512)S(1)} %get-tuple-element.334, f32[512]{0:T(512)S(1)} %get-tuple-element.341, f32[512]{0:T(512)S(1)} %copy-done.74, ...), channel_id=1, replica_groups=mesh['dp'=8,'seq'=4] {'dp','seq'}, use_global_device_ids=true, to_apply=%region_34.35 | all-reduce | flops 3072 | bytes 24576 | tf_op jit(solution)/shard_map/psum | solution.py:294
  451.2 3.3 fusion.120
  454.5 3.8 convolution_add_fusion.3
  458.3 234.8 %all-reduce.4.cloned.1.call-done = (f32[512,1536]{0,1:T(8,128)}, f32[512,512]{1,0:T(8,128)}, f32[512,512]{1,0:T(8,128)}, f32[512,1024]{0,1:T(8,128)}, f32[512,51...) async-done(((f32[512,1536]{0,1:T(8,128)}, f32[512,512]{1,0:T(8,128)}, f32[512,512]{1,0:T(8,128)}, f32[512,1024]{0,1:T(8,128)}, f32[512,512]{1,0:T(8,128)}, ...) | async-done | bytes 16777232 | tf_op jit(solution)/shard_map/psum | solution.py:294
  693.1 3.7 copy.222
  698.6 2.4 copy.327
  (325 shorter events, 128.5 us)
Async XLA Ops:
  7.2 198.6 %copy-start = (bf16[512,2048]{1,0:T(8,128)(2,1)S(1)}, bf16[512,2048]{1,0:T(8,128)(2,1)}, u32[]{:S(2)}) copy-start(bf16[512,2048]{1,0:T(8,128)(2,1)} %param.36) | copy-start | bytes 6291460
  17.9 43.4 %all-to-all-start = ((bf16[2,256,3,4,128]{4,1,2,0,3:T(8,128)(2,1)}), bf16[2,256,3,4,128]{4,1,2,0,3:T(8,128)(2,1)}, u32[]{:S(2)}, u32[]{:S(2)}) async-start(bf16[2,256,3,4,128]{4,1,2,0,3:T(8,128)(2,1)} %copy.196), calls=%async_computation | async-start | bytes 3145728 | tf_op jit(solution)/shard_map/all_to_all | solution.py:128
  65.0 7.0 copy-start.55
  88.4 15.1 %copy-start.5 = (bf16[2,1024,2,64]{1,3,2,0:T(8,128)(2,1)}, bf16[2,1024,2,64]{1,3,2,0:T(8,128)(2,1)S(1)}, u32[]{:S(2)}) copy-start(bf16[2,1024,2,64]{1,3,2,0:T(8,128)(2,1)S(1)} %get-tuple-element.855) | copy-start | bytes 1572868
  88.4 15.1 %copy-start.7 = (bf16[2,1024,2,64]{1,3,2,0:T(8,128)(2,1)}, bf16[2,1024,2,64]{1,3,2,0:T(8,128)(2,1)S(1)}, u32[]{:S(2)}) copy-start(bf16[2,1024,2,64]{1,3,2,0:T(8,128)(2,1)S(1)} %get-tuple-element.856) | copy-start | bytes 1572868
  88.4 15.1 %copy-start.59 = (f32[2,2,1024,1]{2,1,3,0:T(2,128)}, f32[2,2,1024,1]{2,1,3,0:T(2,128)S(1)}, u32[]{:S(2)}) copy-start(f32[2,2,1024,1]{2,1,3,0:T(2,128)S(1)} %get-tuple-element.796) | copy-start | bytes 49156
  90.7 18.2 %all-to-all-start.1 = ((bf16[2,1024,1,128]{3,0,2,1:T(2,128)(2,1)}), bf16[2,1024,1,128]{3,0,2,1:T(2,128)(2,1)}, u32[]{:S(2)}, u32[]{:S(2)}) async-start(bf16[2,1024,1,128]{3,0,2,1:T(2,128)(2,1)} %copy.198), calls=%async_computation.1 | async-start | bytes 1048576 | tf_op jit(solution)/shard_map/all_to_all | solution.py:152
  103.5 14.1 %copy-start.70 = (f32[512]{0:T(512)S(1)}, f32[512]{0:T(512)}, u32[]{:S(2)}) copy-start(f32[512]{0:T(512)} %param.38) | copy-start | bytes 6148
  103.5 14.1 %copy-start.76 = (f32[512]{0:T(512)S(1)}, f32[512]{0:T(512)}, u32[]{:S(2)}) copy-start(f32[512]{0:T(512)} %param.39) | copy-start | bytes 6148
  108.9 29.5 %all-to-all-start.2 = ((bf16[2,256,2,4,128]{4,2,1,0,3:T(2,128)(2,1)}), bf16[2,256,2,4,128]{4,2,1,0,3:T(2,128)(2,1)}, u32[]{:S(2)}, u32[]{:S(2)}) async-start(bf16[2,256,2,4,128]{4,2,1,0,3:T(2,128)(2,1)} %copy.201), calls=%async_computation.2 | async-start | bytes 2097152 | tf_op jit(solution)/shard_map/all_to_all | solution.py:136
  113.2 4.4 copy-start.56
  138.4 18.5 %all-to-all-start.3 = ((bf16[2,256,1,4,128]{4,1,0,2,3:T(8,128)(2,1)}), bf16[2,256,1,4,128]{4,1,0,2,3:T(8,128)(2,1)}, u32[]{:S(2)}, u32[]{:S(2)}) async-start(bf16[2,256,1,4,128]{4,1,0,2,3:T(8,128)(2,1)} %copy.203), calls=%async_computation.3 | async-start | bytes 1048576 | tf_op jit(solution)/shard_map/all_to_all | solution.py:170
  142.9 19.2 %copy-start.58 = (s32[2,1024]{1,0:T(2,128)S(1)}, s32[2,1024]{1,0:T(2,128)}, u32[]{:S(2)}) copy-start(s32[2,1024]{1,0:T(2,128)} %param.29) | copy-start | bytes 24580
  162.1 25.4 %copy-start.69 = (f32[512]{0:T(512)S(1)}, f32[512]{0:T(512)}, u32[]{:S(2)}) copy-start(f32[512]{0:T(512)} %param.42) | copy-start | bytes 6148
  182.6 23.2 %copy-start.65 = (f32[512]{0:T(512)S(1)}, f32[512]{0:T(512)}, u32[]{:S(2)}) copy-start(f32[512]{0:T(512)} %param.40) | copy-start | bytes 6148
  182.6 23.2 %copy-start.67 = (f32[512]{0:T(512)S(1)}, f32[512]{0:T(512)}, u32[]{:S(2)}) copy-start(f32[512]{0:T(512)} %param.41) | copy-start | bytes 6148
  182.6 18.9 %all-to-all-start.4 = ((bf16[2,1024,1,128]{3,0,2,1:T(2,128)(2,1)}), bf16[2,1024,1,128]{3,0,2,1:T(2,128)(2,1)}, u32[]{:S(2)}, u32[]{:S(2)}) async-start(bf16[2,1024,1,128]{3,0,2,1:T(2,128)(2,1)} %copy.205), calls=%async_computation.4 | async-start | bytes 1048576 | tf_op jit(solution)/shard_map/all_to_all | solution.py:183
  205.5 10.1 %copy-start.2 = (f32[512,512]{1,0:T(8,128)}, f32[512,512]{1,0:T(8,128)S(1)}, u32[]{:S(2)}) copy-start(f32[512,512]{1,0:T(8,128)S(1)} %get-tuple-element.451) | copy-start | bytes 3145732
  205.5 10.1 %copy-start.61 = (f32[512]{0:T(512)}, f32[512]{0:T(512)S(1)}, u32[]{:S(2)}) copy-start(f32[512]{0:T(512)S(1)} %broadcast_multiply_fusion.6) | copy-start | bytes 6148
  205.8 9.8 %copy-start.63 = (f32[512]{0:T(512)}, f32[512]{0:T(512)S(1)}, u32[]{:S(2)}) copy-start(f32[512]{0:T(512)S(1)} %add_rsqrt_fusion.1) | copy-start | bytes 6148
  207.5 4.0 copy-start.25
  207.5 2.8 copy-start.73
  216.0 29.8 %copy-start.10 = (f32[512,512]{1,0:T(8,128)}, f32[512,512]{1,0:T(8,128)S(1)}, u32[]{:S(2)}) copy-start(f32[512,512]{1,0:T(8,128)S(1)} %subtract_multiply_fusion.1) | copy-start | bytes 3145732
  216.0 30.6 %copy-start.4 = (bf16[2,1024,2,64]{1,3,2,0:T(8,128)(2,1)S(1)}, bf16[2,1024,2,64]{1,3,2,0:T(8,128)(2,1)}, u32[]{:S(2)}) copy-start(bf16[2,1024,2,64]{1,3,2,0:T(8,128)(2,1)} %get-tuple-element.854) | copy-start | bytes 1572868
  216.0 30.6 %copy-start.9 = (bf16[2,1024,2,64]{1,3,2,0:T(8,128)(2,1)S(1)}, bf16[2,1024,2,64]{1,3,2,0:T(8,128)(2,1)}, u32[]{:S(2)}) copy-start(bf16[2,1024,2,64]{1,3,2,0:T(8,128)(2,1)} %get-tuple-element.857) | copy-start | bytes 1572868
  221.2 18.4 %all-to-all-start.5 = ((bf16[2,256,4,128]{3,1,0,2:T(8,128)(2,1)}), bf16[2,256,4,128]{3,1,0,2:T(8,128)(2,1)}, u32[]{:S(2)}, u32[]{:S(2)}) async-start(bf16[2,256,4,128]{3,1,0,2:T(8,128)(2,1)} %copy.208), calls=%async_computation.5 | async-start | bytes 1048576 | tf_op jit(solution)/shard_map/all_to_all | solution.py:218
  251.6 2.7 copy-start.32
  255.2 4.1 copy-start.33
  265.2 2.7 copy-start.32
  268.8 4.1 copy-start.33
  273.7 18.3 %copy-start.11 = (f32[512,512]{1,0:T(8,128)S(1)}, f32[512,512]{1,0:T(8,128)}, u32[]{:S(2)}) copy-start(f32[512,512]{1,0:T(8,128)} %copy-done.10) | copy-start | bytes 3145732
  291.6 2.9 copy-start.50
  294.5 5.7 copy-start.13
  296.0 17.8 %all-to-all-start.7 = ((bf16[2,256,4,128]{3,1,0,2:T(8,128)(2,1)}), bf16[2,256,4,128]{3,1,0,2:T(8,128)(2,1)}, u32[]{:S(2)}, u32[]{:S(2)}) async-start(bf16[2,256,4,128]{3,1,0,2:T(8,128)(2,1)} %copy.213), calls=%async_computation.7 | async-start | bytes 1048576 | tf_op jit(solution)/shard_map/all_to_all | solution.py:265
  301.4 21.9 %copy-start.6 = (bf16[2,1024,2,64]{1,3,2,0:T(8,128)(2,1)S(1)}, bf16[2,1024,2,64]{1,3,2,0:T(8,128)(2,1)}, u32[]{:S(2)}) copy-start(bf16[2,1024,2,64]{1,3,2,0:T(8,128)(2,1)} %copy-done.5) | copy-start | bytes 1572868
  301.4 21.9 %copy-start.8 = (bf16[2,1024,2,64]{1,3,2,0:T(8,128)(2,1)S(1)}, bf16[2,1024,2,64]{1,3,2,0:T(8,128)(2,1)}, u32[]{:S(2)}) copy-start(bf16[2,1024,2,64]{1,3,2,0:T(8,128)(2,1)} %copy-done.7) | copy-start | bytes 1572868
  301.5 21.9 %copy-start.60 = (f32[2,2,1024,1]{2,1,3,0:T(2,128)S(1)}, f32[2,2,1024,1]{2,1,3,0:T(2,128)}, u32[]{:S(2)}) copy-start(f32[2,2,1024,1]{2,1,3,0:T(2,128)} %copy-done.59) | copy-start | bytes 49156
  313.7 44.5 %all-to-all-start.9 = ((bf16[2,1024,2,1,128]{4,0,3,2,1:T(2,128)(2,1)}), bf16[2,1024,2,1,128]{4,0,3,2,1:T(2,128)(2,1)}, u32[]{:S(2)}, u32[]{:S(2)}) async-start(bf16[2,1024,2,1,128]{4,0,3,2,1:T(2,128)(2,1)} %copy.218), calls=%async_computation.9 | async-start | bytes 2097152 | tf_op jit(solution)/shard_map/all_to_all | solution.py:249
  328.4 2.7 copy-start.38
  332.0 4.1 copy-start.39
  333.5 2.6 copy-start.41
  341.9 2.7 copy-start.38
  345.5 4.1 copy-start.39
  350.4 13.3 %copy-start.12 = (f32[512,512]{1,0:T(8,128)S(1)}, f32[512,512]{1,0:T(8,128)}, u32[]{:S(2)}) copy-start(f32[512,512]{1,0:T(8,128)} %copy-done.10) | copy-start | bytes 3145732
  353.2 13.0 %copy-start.3 = (f32[512,512]{1,0:T(8,128)S(1)}, f32[512,512]{1,0:T(8,128)}, u32[]{:S(2)}) copy-start(f32[512,512]{1,0:T(8,128)} %copy-done.2) | copy-start | bytes 3145732
  353.2 13.0 %copy-start.62 = (f32[512]{0:T(512)S(1)}, f32[512]{0:T(512)}, u32[]{:S(2)}) copy-start(f32[512]{0:T(512)} %copy-done.61) | copy-start | bytes 6148
  353.2 13.0 %copy-start.64 = (f32[512]{0:T(512)S(1)}, f32[512]{0:T(512)}, u32[]{:S(2)}) copy-start(f32[512]{0:T(512)} %copy-done.63) | copy-start | bytes 6148
  353.2 13.0 %copy-start.66 = (f32[512]{0:T(512)S(1)}, f32[512]{0:T(512)}, u32[]{:S(2)}) copy-start(f32[512]{0:T(512)} %param.40) | copy-start | bytes 6148
  353.2 13.0 %copy-start.68 = (f32[512]{0:T(512)S(1)}, f32[512]{0:T(512)}, u32[]{:S(2)}) copy-start(f32[512]{0:T(512)} %param.41) | copy-start | bytes 6148
  358.2 41.1 %all-to-all-start.8 = ((bf16[2,1024,3,1,128]{4,0,3,2,1:T(2,128)(2,1)}), bf16[2,1024,3,1,128]{4,0,3,2,1:T(2,128)(2,1)}, u32[]{:S(2)}, u32[]{:S(2)}) async-start(bf16[2,1024,3,1,128]{4,0,3,2,1:T(2,128)(2,1)} %copy.215), calls=%async_computation.8 | async-start | bytes 3145728 | tf_op jit(solution)/shard_map/all_to_all | solution.py:287
  363.3 329.8 %all-reduce.4.cloned.1.call-start = ((), (), s32[]{:S(2)}) async-start(), calls=%async_computation.10 | async-start | bytes 33554432 | tf_op jit(solution)/shard_map/psum | solution.py:294
  366.2 5.2 copy-start.26
  366.2 5.2 copy-start.53
  371.4 3.5 copy-start.14
  371.4 3.5 copy-start.22
  371.4 4.9 copy-start.30
  371.4 4.9 copy-start.77
  376.3 4.6 copy-start.57
  383.1 23.1 %copy-start.51 = (bf16[2,256,512]{2,1,0:T(8,128)(2,1)S(1)}, bf16[2,256,512]{2,1,0:T(8,128)(2,1)}, u32[]{:S(2)}) copy-start(bf16[2,256,512]{2,1,0:T(8,128)(2,1)} %param.26) | copy-start | bytes 1572868
  693.1 3.7 copy-start.31
  696.7 6.5 copy-start.54
  698.6 5.7 copy-start.28
  704.2 3.7 copy-start.27
  704.2 5.7 copy-start.1
  (47 other events, 77.2 us)
Sparse Core Ops, SparseCore 0:
  409.0 284.0 all-reduce.3
where the time goes:
time: 728 us; the launch traced here: 717 us
  waiting for transfers between devices  351 us (48%)
  local copies, waits for them, and re-layouts  112 us (15%)
  matrix products  105 us (14%)
  blocking collectives  56.5 us (8%)
  starting transfers between devices  42.4 us (6%)
  other arithmetic  33.6 us (5%)
  between operations  14.9 us (2%)
    psum x1, waiting for transfers between devices, body(): lax.psum((grad_qkv, grad_self_out, grad_cross_q, grad_cross_kv, grad_cros...  235 us
    psum x1, blocking collectives, body(): lax.psum((grad_qkv, grad_self_out, grad_cross_q, grad_cross_kv, grad_cros...  40.1 us
    all_to_all x1, waiting for transfers between devices, body(): lax.all_to_all(mixed_proj, 'seq', split_axis=3, concat_axis=1, tiled=True)  37.1 us
    unnamed x122, local copies, waits for them, and re-layouts  19.7 us
    dot_general x7, matrix products, left_dot(): lax.dot_general(left, right, (((0,), (0,)), ((), ())), preferred_element_...  19 us
    all_to_all x1, blocking collectives, body(): lax.all_to_all(d_cross_q.reshape(row_count, seq_len, 1, 1, head_share), '...  16.4 us
    all_to_all x1, waiting for transfers between devices, body(): lax.all_to_all(d_mixed, 'seq', split_axis=1, concat_axis=3, tiled=True)  16.2 us
    all_to_all x1, waiting for transfers between devices, body(): lax.all_to_all(memory_proj, 'seq', split_axis=3, concat_axis=1, tiled=True)  15.7 us
  transfers between devices with their start and end apart: 10, of which 9 were waited for; matrix products, arithmetic and copies ran while one was open for 14% of the time, Pallas kernels for 0%

commit v1 on v0

--- a/solution.py
+++ b/solution.py
@@ -5,6 +5,29 @@
 from jax.sharding import PartitionSpec as P
 
 HEAD_DIM = 64
+
+
+def cut_along(x, dim, count):
+    shape = x.shape
+    tiles = x.reshape(*shape[:dim], count, shape[dim] // count, *shape[dim + 1 :])
+    return jnp.moveaxis(tiles, dim, 0)
+
+
+def in_order(blocks, dim):
+    dims = list(blocks.shape[1:])
+    dims[dim] *= blocks.shape[0]
+    return jnp.moveaxis(blocks, 0, dim).reshape(dims)
+
+
+def rotated_exchange(x, axis, split_dim, concat_dim):
+    peers, position = (lax.axis_size(axis), lax.axis_index(axis))
+    pieces = cut_along(x, split_dim, peers)
+    outs = [pieces[position]]
+    for step in range(1, peers):
+        sent = pieces[(position + step) % peers]
+        outs.append(lax.ppermute(sent, axis, [(i, (i + step) % peers) for i in range(peers)]))
+    pieces = jnp.stack(outs)[(position - jnp.arange(peers)) % peers]
+    return in_order(pieces, concat_dim)
 
 
 def mat_dot(left, right):
@@ -125,7 +148,7 @@
         .astype(jnp.bfloat16)
         .reshape(row_count, tok_local, 3, seq_parts, head_share)
     )
-    self_heads = lax.all_to_all(mixed_proj, "seq", split_axis=3, concat_axis=1, tiled=True).reshape(
+    self_heads = rotated_exchange(mixed_proj, "seq", 3, 1).reshape(
         row_count, seq_len, 3, heads_here, HEAD_DIM
     )
     memory_proj = (

time: 728 us -> 737 us (1.012)
    all_to_all x1 -> x0, waiting for transfers between devices: 37.1 us -> none  [body(): lax.all_to_all(mixed_proj, 'seq', split_axis=3, concat_axis=1, tiled=True)]
    ppermute x0 -> x3, waiting for transfers between devices: none -> 31.1 us  [rotated_exchange(): lax.ppermute(sent, axis, [(i, (i + step) % peers) for i in range(peers)])]
    another operation x10 -> x13, local copies, waits for them, and re-layouts: 6.96 us -> 21.2 us
    reshape x3 -> x0, local copies, waits for them, and re-layouts: 10.6 us -> none  [the longest x2 6.83 us: body(): mixed_proj = mat_dot(flat_tokens, w_qkv).astype(jnp.bfloat16).reshape(row...]
    unnamed x122 -> x120, local copies, waits for them, and re-layouts: 19.7 us -> 22.2 us
  transfers between devices with their start and end apart: 10 -> 12, of which waited for: 9 -> 10; matrix products, arithmetic and copies ran while one was open for 14% -> 13% of each run, Pallas kernels for 0% -> 0%
where the time goes in v1:
time: 737 us; the launch traced here: 727 us
  waiting for transfers between devices  348 us (47%)
  local copies, waits for them, and re-layouts  119 us (16%)
  matrix products  109 us (15%)
  blocking collectives  56.5 us (8%)
  starting transfers between devices  42.7 us (6%)
  other arithmetic  36.1 us (5%)
  between operations  15 us (2%)
    psum x1, waiting for transfers between devices, body(): lax.psum((grad_qkv, grad_self_out, grad_cross_q, grad_cross_kv, grad_cros...  235 us
    psum x1, blocking collectives, body(): lax.psum((grad_qkv, grad_self_out, grad_cross_q, grad_cross_kv, grad_cros...  40.1 us
    ppermute x3, waiting for transfers between devices, rotated_exchange(): lax.ppermute(sent, axis, [(i, (i + step) % peers) for i in range(peers)])  31.1 us
    unnamed x120, local copies, waits for them, and re-layouts  22.2 us
    dot_general x7, matrix products, left_dot(): lax.dot_general(left, right, (((0,), (0,)), ((), ())), preferred_element_...  19 us
    dot_general x8, matrix products, masked_scores(): jnp.einsum('qhd,khd->hqk', queries, key_heads, preferred_element_type=jnp...  16.9 us
    all_to_all x1, blocking collectives, body(): lax.all_to_all(d_cross_q.reshape(row_count, seq_len, 1, 1, head_share), '...  16.4 us
    all_to_all x1, waiting for transfers between devices, body(): lax.all_to_all(d_mixed, 'seq', split_axis=1, concat_axis=3, tiled=True)  16.2 us
  transfers between devices with their start and end apart: 12, of which 10 were waited for; matrix products, arithmetic and copies ran while one was open for 13% of the time, Pallas kernels for 0%

profile of v1, /device:TPU:0, one launch (start us, length us, event | category | flops | bytes accessed | tf_op | source)
XLA Modules:
  0.0 727.0 jit_solution(14503125099861639045)
XLA Ops:
  7.2 3.8 convolution_convert_fusion
  11.1 3.9 reshape_reshape.6
  15.0 6.5 constant_dynamic-slice_fusion.9
  22.3 5.0 collective-permute-start.2
  30.1 7.2 collective-permute-done.2
  37.3 23.9 %collective-permute-done.1 = bf16[2,256,3,1,128]{4,1,2,0,3:T(8,128)(2,1)} collective-permute-done((bf16[2,256,3,1,128]{4,1,2,0,3:T(8,128)(2,1)}, bf16[2,256,3,1,128]{4,1,2,0,3:T(8,128)(2,1)}, u32[]{:S(2)}, u32[]{:S(2)}) %collective-permute-start.1) | collective-permute-done | bytes 393248 | tf_op jit(solution)/shard_map/ppermute | solution.py:28
  63.7 3.3 gather_fusion
  67.0 3.8 copy.198
  70.7 3.8 reshape_reshape.7
  74.5 2.5 slice_bitcast_fusion.2
  77.9 18.4 %while.52 = (s32[]{:T(128)}, bf16[2,1024,2,64]{1,3,2,0:T(8,128)(2,1)}, f32[2,2,1024,1]{2,1,3,0:T(2,128)S(1)}, bf16[2,1024,2,64]{1,3,2,0:T(8,128)(2,1)}, s32[2,10...) while((s32[]{:T(128)}, ...), condition=%wide.region_3.4_spmd, body=%wide.region_0.3_spmd.sunk | while | flops 565311488 | bytes 36780216 | solution.py:174
  78.6 2.9 fusion.227
  83.5 2.8 fusion.229
  87.7 2.9 fusion.227
  92.7 2.8 fusion.229
  98.3 5.1 all-to-all-start
  103.4 3.1 convolution_convert_fusion.1
  110.1 8.6 %all-to-all-done = bf16[2,1024,1,128]{3,0,2,1:T(2,128)(2,1)} async-done(((bf16[2,1024,1,128]{3,0,2,1:T(2,128)(2,1)}), bf16[2,1024,1,128]{3,0,2,1:T(2,128)(2,1)}, u32[]{:S(2)}, u32[]{:S(2)}) %all-to-all-start) | async-done | bytes 524320 | tf_op jit(solution)/shard_map/all_to_all | solution.py:175
  118.7 4.2 all-to-all-start.1
  133.5 15.3 %all-to-all-done.1 = bf16[2,256,2,4,128]{4,2,1,0,3:T(2,128)(2,1)} async-done(((bf16[2,256,2,4,128]{4,2,1,0,3:T(2,128)(2,1)}), bf16[2,256,2,4,128]{4,2,1,0,3:T(2,128)(2,1)}, u32[]{:S(2)}, u32[]{:S(2)}) %all-to-all-start.1) | async-done | bytes 1048608 | tf_op jit(solution)/shard_map/all_to_all | solution.py:159
  148.8 4.1 all-to-all-start.2
  153.0 3.8 copy.203
  156.8 2.6 reshape.454
  161.6 5.4 all-to-all-done.2
  172.2 18.5 %while.53 = (s32[]{:T(128)}, bf16[2,1024,2,64]{1,3,2,0:T(8,128)(2,1)}, f32[2,2,1024,1]{2,1,3,0:T(2,128)S(1)}, bf16[2,1024,2,64]{1,3,2,0:T(8,128)(2,1)}, s32[2,10...) while((s32[]{:T(128)}, ...), condition=%wide.region_9.10_spmd, body=%wide.region_6.9_spmd.sunk | while | flops 563214336 | bytes 36792512 | solution.py:203
  172.9 2.9 fusion.231
  177.8 2.8 fusion.233
  182.1 2.9 fusion.231
  187.1 2.8 fusion.233
  192.7 4.8 all-to-all-start.3
  199.4 12.1 %all-to-all-done.3 = bf16[2,1024,1,128]{3,0,2,1:T(2,128)(2,1)} async-done(((bf16[2,1024,1,128]{3,0,2,1:T(2,128)(2,1)}), bf16[2,1024,1,128]{3,0,2,1:T(2,128)(2,1)}, u32[]{:S(2)}, u32[]{:S(2)}) %all-to-all-start.3) | async-done | bytes 524320 | tf_op jit(solution)/shard_map/all_to_all | solution.py:206
  231.3 4.3 all-to-all-start.4
  235.6 14.1 %all-to-all-done.4 = bf16[2,256,4,128]{3,1,0,2:T(8,128)(2,1)} async-done(((bf16[2,256,4,128]{3,1,0,2:T(8,128)(2,1)}), bf16[2,256,4,128]{3,1,0,2:T(8,128)(2,1)}, u32[]{:S(2)}, u32[]{:S(2)}) %all-to-all-start.4) | async-done | bytes 524320 | tf_op jit(solution)/shard_map/all_to_all | solution.py:241
  256.6 27.1 %while.54 = (s32[]{:T(128)}, bf16[2,1024,2,64]{1,3,2,0:T(8,128)(2,1)}, bf16[2,1024,2,64]{1,3,2,0:T(8,128)(2,1)}, bf16[2,1024,2,64]{1,3,2,0:T(8,128)(2,1)}, bf16[...) while((s32[]{:T(128)}, ...), condition=%wide.region_20.21_spmd, body=%wide.region_18.20_spmd.sunk | while | flops 1375336448 | bytes 86594928 | solution.py:257
  258.7 3.0 multiply_reduce_fusion.13
  261.7 2.7 multiply_convert_fusion.8
  266.8 2.5 fusion.245
  272.2 3.0 multiply_reduce_fusion.13
  275.2 2.7 multiply_convert_fusion.8
  280.4 2.5 fusion.245
  285.2 16.4 %all_to_all.135 = bf16[2,1024,1,1,128]{4,0,3,2,1:T(2,128)(2,1)S(1)} all-to-all(bf16[2,1024,1,1,128]{4,0,3,2,1:T(2,128)(2,1)S(1)} %copy.211), channel_id=1, replica_groups=mesh['dp'=8,'seq'=4] {'seq'}, dimensions={1} | all-to-all | bytes 1048576 | tf_op jit(solution)/shard_map/all_to_all | solution.py:265
  306.0 4.1 all-to-all-start.6
  313.6 10.2 %all-to-all-done.6 = bf16[2,256,4,128]{3,1,0,2:T(8,128)(2,1)} async-done(((bf16[2,256,4,128]{3,1,0,2:T(8,128)(2,1)}), bf16[2,256,4,128]{3,1,0,2:T(8,128)(2,1)}, u32[]{:S(2)}, u32[]{:S(2)}) %all-to-all-start.6) | async-done | bytes 524320 | tf_op jit(solution)/shard_map/all_to_all | solution.py:288
  323.8 4.5 all-to-all-start.8
  333.4 27.0 %while.55 = (s32[]{:T(128)}, bf16[2,1024,2,64]{1,3,2,0:T(8,128)(2,1)}, bf16[2,1024,2,64]{1,3,2,0:T(8,128)(2,1)}, bf16[2,1024,2,64]{1,3,2,0:T(8,128)(2,1)}, bf16[...) while((s32[]{:T(128)}, ...), condition=%wide.region_25.26_spmd, body=%wide.region_23.25_spmd.sunk | while | flops 1377433600 | bytes 86582632 | solution.py:304
  335.4 3.0 multiply_reduce_fusion.14
  338.4 2.7 multiply_convert_fusion.9
  343.6 2.5 fusion.258
  348.9 3.0 multiply_reduce_fusion.14
  351.9 2.7 multiply_convert_fusion.9
  357.1 2.5 fusion.258
  360.4 2.8 pad_maximum_fusion
  363.2 5.0 copy.216
  368.2 5.1 all-to-all-start.7
  376.3 5.2 fusion.155
  381.5 3.5 fusion.150
  393.1 16.2 %all-to-all-done.7 = bf16[2,1024,3,1,128]{4,0,3,2,1:T(2,128)(2,1)} async-done(((bf16[2,1024,3,1,128]{4,0,3,2,1:T(2,128)(2,1)}), bf16[2,1024,3,1,128]{4,0,3,2,1:T(2,128)(2,1)}, u32[]{:S(2)}, u32[]{:S(2)}) %all-to-all-start.7) | async-done | bytes 1572896 | tf_op jit(solution)/shard_map/all_to_all | solution.py:310
  413.3 2.8 reshape.466
  416.1 2.7 convolution_bitcast_fusion
  419.6 40.1 %all-reduce = (f32[512]{0:T(512)}, f32[512]{0:T(512)}, f32[512]{0:T(512)}, f32[512]{0:T(512)}, f32[512]{0:T(512)}, /*index=5*/f32[512]{0:T(512)}) all-reduce(f32[512]{0:T(512)S(1)} %get-tuple-element.318, f32[512]{0:T(512)S(1)} %get-tuple-element.325, f32[512]{0:T(512)S(1)} %copy-done.71, ...), channel_id=1, replica_groups=mesh['dp'=8,'seq'=4] {'dp','seq'}, use_global_device_ids=true, to_apply=%region_34.35 | all-reduce | flops 3072 | bytes 24576 | tf_op jit(solution)/shard_map/psum | solution.py:317
  461.2 3.3 fusion.120
  464.5 3.8 convolution_add_fusion.3
  468.3 234.8 %all-reduce.4.cloned.1.call-done = (f32[512,1536]{0,1:T(8,128)}, f32[512,512]{1,0:T(8,128)}, f32[512,512]{1,0:T(8,128)}, f32[512,1024]{0,1:T(8,128)}, f32[512,51...) async-done(((f32[512,1536]{0,1:T(8,128)}, f32[512,512]{1,0:T(8,128)}, f32[512,512]{1,0:T(8,128)}, f32[512,1024]{0,1:T(8,128)}, f32[512,512]{1,0:T(8,128)}, ...) | async-done | bytes 16777232 | tf_op jit(solution)/shard_map/psum | solution.py:317
  703.1 3.7 copy.223
  (331 shorter events, 139.8 us)
Async XLA Ops:
  7.2 208.7 %copy-start = (bf16[512,2048]{1,0:T(8,128)(2,1)S(1)}, bf16[512,2048]{1,0:T(8,128)(2,1)}, u32[]{:S(2)}) copy-start(bf16[512,2048]{1,0:T(8,128)(2,1)} %param.36) | copy-start | bytes 6291460
  22.3 15.0 %collective-permute-start.2 = (bf16[2,256,3,1,128]{4,1,2,0,3:T(8,128)(2,1)}, bf16[2,256,3,1,128]{4,1,2,0,3:T(8,128)(2,1)S(1)}, u32[]{:S(2)}, u32[]{:S(2)}) collective-permute-start(bf16[2,256,3,1,128]{4,1,2,0,3:T(8,128)(2,1)} %bitcast.305), channel_id=1, source_target_pairs={{0,3},{1,0},{2,1},{3,2},{4,7},{5,4},{6,5},{7,6},{8,11},{9,8},{10,9... | collective-permute-start | bytes 1179656 | tf_op jit(solution)/shard_map/ppermute | solution.py:28
  28.2 33.0 %collective-permute-start.1 = (bf16[2,256,3,1,128]{4,1,2,0,3:T(8,128)(2,1)}, bf16[2,256,3,1,128]{4,1,2,0,3:T(8,128)(2,1)}, u32[]{:S(2)}, u32[]{:S(2)}) collective-permute-start(bf16[2,256,3,1,128]{4,1,2,0,3:T(8,128)(2,1)} %bitcast.306), channel_id=1, source_target_pairs={{0,2},{1,3},{2,0},{3,1},{4,6},{5,7},{6,4},{7,5},{8,10},{9,11},{10,... | collective-permute-start | bytes 1179656 | tf_op jit(solution)/shard_map/ppermute | solution.py:28
  29.0 32.2 %collective-permute-start = (bf16[2,256,3,1,128]{4,1,2,0,3:T(8,128)(2,1)}, bf16[2,256,3,1,128]{4,1,2,0,3:T(8,128)(2,1)}, u32[]{:S(2)}, u32[]{:S(2)}) collective-permute-start(bf16[2,256,3,1,128]{4,1,2,0,3:T(8,128)(2,1)} %bitcast.307), channel_id=1, source_target_pairs={{0,1},{1,2},{2,3},{3,0},{4,5},{5,6},{6,7},{7,4},{8,9},{9,10},{10,1... | collective-permute-start | bytes 1179656 | tf_op jit(solution)/shard_map/ppermute | solution.py:28
  70.7 7.2 copy-start.53
  96.3 13.8 %copy-start.56 = (f32[2,2,1024,1]{2,1,3,0:T(2,128)}, f32[2,2,1024,1]{2,1,3,0:T(2,128)S(1)}, u32[]{:S(2)}) copy-start(f32[2,2,1024,1]{2,1,3,0:T(2,128)S(1)} %get-tuple-element.784) | copy-start | bytes 49156
  98.3 20.4 %all-to-all-start = ((bf16[2,1024,1,128]{3,0,2,1:T(2,128)(2,1)}), bf16[2,1024,1,128]{3,0,2,1:T(2,128)(2,1)}, u32[]{:S(2)}, u32[]{:S(2)}) async-start(bf16[2,1024,1,128]{3,0,2,1:T(2,128)(2,1)} %copy.199), calls=%async_computation | async-start | bytes 1048576 | tf_op jit(solution)/shard_map/all_to_all | solution.py:175
  110.1 17.2 %copy-start.67 = (f32[512]{0:T(512)S(1)}, f32[512]{0:T(512)}, u32[]{:S(2)}) copy-start(f32[512]{0:T(512)} %param.38) | copy-start | bytes 6148
  110.1 17.2 %copy-start.73 = (f32[512]{0:T(512)S(1)}, f32[512]{0:T(512)}, u32[]{:S(2)}) copy-start(f32[512]{0:T(512)} %param.39) | copy-start | bytes 6148
  118.7 30.1 %all-to-all-start.1 = ((bf16[2,256,2,4,128]{4,2,1,0,3:T(2,128)(2,1)}), bf16[2,256,2,4,128]{4,2,1,0,3:T(2,128)(2,1)}, u32[]{:S(2)}, u32[]{:S(2)}) async-start(bf16[2,256,2,4,128]{4,2,1,0,3:T(2,128)(2,1)} %copy.202), calls=%async_computation.1 | async-start | bytes 2097152 | tf_op jit(solution)/shard_map/all_to_all | solution.py:159
  148.8 18.2 %all-to-all-start.2 = ((bf16[2,256,1,4,128]{4,1,0,2,3:T(8,128)(2,1)}), bf16[2,256,1,4,128]{4,1,0,2,3:T(8,128)(2,1)}, u32[]{:S(2)}, u32[]{:S(2)}) async-start(bf16[2,256,1,4,128]{4,1,0,2,3:T(8,128)(2,1)} %copy.204), calls=%async_computation.2 | async-start | bytes 1048576 | tf_op jit(solution)/shard_map/all_to_all | solution.py:193
  152.9 19.2 %copy-start.55 = (s32[2,1024]{1,0:T(2,128)S(1)}, s32[2,1024]{1,0:T(2,128)}, u32[]{:S(2)}) copy-start(s32[2,1024]{1,0:T(2,128)} %param.29) | copy-start | bytes 24580
  172.2 25.3 %copy-start.66 = (f32[512]{0:T(512)S(1)}, f32[512]{0:T(512)}, u32[]{:S(2)}) copy-start(f32[512]{0:T(512)} %param.42) | copy-start | bytes 6148
  192.7 23.1 %copy-start.62 = (f32[512]{0:T(512)S(1)}, f32[512]{0:T(512)}, u32[]{:S(2)}) copy-start(f32[512]{0:T(512)} %param.40) | copy-start | bytes 6148
  192.7 23.2 %copy-start.64 = (f32[512]{0:T(512)S(1)}, f32[512]{0:T(512)}, u32[]{:S(2)}) copy-start(f32[512]{0:T(512)} %param.41) | copy-start | bytes 6148
  192.7 18.8 %all-to-all-start.3 = ((bf16[2,1024,1,128]{3,0,2,1:T(2,128)(2,1)}), bf16[2,1024,1,128]{3,0,2,1:T(2,128)(2,1)}, u32[]{:S(2)}, u32[]{:S(2)}) async-start(bf16[2,1024,1,128]{3,0,2,1:T(2,128)(2,1)} %copy.206), calls=%async_computation.3 | async-start | bytes 1048576 | tf_op jit(solution)/shard_map/all_to_all | solution.py:206
  215.5 10.1 %copy-start.2 = (f32[512,512]{1,0:T(8,128)}, f32[512,512]{1,0:T(8,128)S(1)}, u32[]{:S(2)}) copy-start(f32[512,512]{1,0:T(8,128)S(1)} %get-tuple-element.439) | copy-start | bytes 3145732
  215.6 10.1 %copy-start.58 = (f32[512]{0:T(512)}, f32[512]{0:T(512)S(1)}, u32[]{:S(2)}) copy-start(f32[512]{0:T(512)S(1)} %broadcast_multiply_fusion.6) | copy-start | bytes 6148
  215.9 9.8 %copy-start.60 = (f32[512]{0:T(512)}, f32[512]{0:T(512)S(1)}, u32[]{:S(2)}) copy-start(f32[512]{0:T(512)S(1)} %add_rsqrt_fusion.1) | copy-start | bytes 6148
  217.5 4.0 copy-start.23
  217.5 2.8 copy-start.70
  226.1 29.7 %copy-start.8 = (f32[512,512]{1,0:T(8,128)}, f32[512,512]{1,0:T(8,128)S(1)}, u32[]{:S(2)}) copy-start(f32[512,512]{1,0:T(8,128)S(1)} %subtract_multiply_fusion.1) | copy-start | bytes 3145732
  226.1 30.6 %copy-start.4 = (bf16[2,1024,2,64]{1,3,2,0:T(8,128)(2,1)S(1)}, bf16[2,1024,2,64]{1,3,2,0:T(8,128)(2,1)}, u32[]{:S(2)}) copy-start(bf16[2,1024,2,64]{1,3,2,0:T(8,128)(2,1)} %get-tuple-element.842) | copy-start | bytes 1572868
  226.1 30.6 %copy-start.7 = (bf16[2,1024,2,64]{1,3,2,0:T(8,128)(2,1)S(1)}, bf16[2,1024,2,64]{1,3,2,0:T(8,128)(2,1)}, u32[]{:S(2)}) copy-start(bf16[2,1024,2,64]{1,3,2,0:T(8,128)(2,1)} %get-tuple-element.845) | copy-start | bytes 1572868
  231.3 18.4 %all-to-all-start.4 = ((bf16[2,256,4,128]{3,1,0,2:T(8,128)(2,1)}), bf16[2,256,4,128]{3,1,0,2:T(8,128)(2,1)}, u32[]{:S(2)}, u32[]{:S(2)}) async-start(bf16[2,256,4,128]{3,1,0,2:T(8,128)(2,1)} %copy.209), calls=%async_computation.4 | async-start | bytes 1048576 | tf_op jit(solution)/shard_map/all_to_all | solution.py:241
  261.7 2.7 copy-start.30
  265.3 4.1 copy-start.31
  275.2 2.7 copy-start.30
  278.8 4.1 copy-start.31
  280.4 2.6 copy-start.43
  283.8 18.3 %copy-start.9 = (f32[512,512]{1,0:T(8,128)S(1)}, f32[512,512]{1,0:T(8,128)}, u32[]{:S(2)}) copy-start(f32[512,512]{1,0:T(8,128)} %copy-done.8) | copy-start | bytes 3145732
  301.6 2.9 copy-start.48
  304.5 5.7 copy-start.11
  306.0 17.8 %all-to-all-start.6 = ((bf16[2,256,4,128]{3,1,0,2:T(8,128)(2,1)}), bf16[2,256,4,128]{3,1,0,2:T(8,128)(2,1)}, u32[]{:S(2)}, u32[]{:S(2)}) async-start(bf16[2,256,4,128]{3,1,0,2:T(8,128)(2,1)} %copy.214), calls=%async_computation.6 | async-start | bytes 1048576 | tf_op jit(solution)/shard_map/all_to_all | solution.py:288
  311.5 21.9 %copy-start.5 = (bf16[2,1024,2,64]{1,3,2,0:T(8,128)(2,1)S(1)}, bf16[2,1024,2,64]{1,3,2,0:T(8,128)(2,1)}, u32[]{:S(2)}) copy-start(bf16[2,1024,2,64]{1,3,2,0:T(8,128)(2,1)} %get-tuple-element.843) | copy-start | bytes 1572868
  311.5 21.9 %copy-start.6 = (bf16[2,1024,2,64]{1,3,2,0:T(8,128)(2,1)S(1)}, bf16[2,1024,2,64]{1,3,2,0:T(8,128)(2,1)}, u32[]{:S(2)}) copy-start(bf16[2,1024,2,64]{1,3,2,0:T(8,128)(2,1)} %get-tuple-element.844) | copy-start | bytes 1572868
  311.5 21.9 %copy-start.57 = (f32[2,2,1024,1]{2,1,3,0:T(2,128)S(1)}, f32[2,2,1024,1]{2,1,3,0:T(2,128)}, u32[]{:S(2)}) copy-start(f32[2,2,1024,1]{2,1,3,0:T(2,128)} %copy-done.56) | copy-start | bytes 49156
  323.8 44.4 %all-to-all-start.8 = ((bf16[2,1024,2,1,128]{4,0,3,2,1:T(2,128)(2,1)}), bf16[2,1024,2,1,128]{4,0,3,2,1:T(2,128)(2,1)}, u32[]{:S(2)}, u32[]{:S(2)}) async-start(bf16[2,1024,2,1,128]{4,0,3,2,1:T(2,128)(2,1)} %copy.219), calls=%async_computation.8 | async-start | bytes 2097152 | tf_op jit(solution)/shard_map/all_to_all | solution.py:272
  338.4 2.7 copy-start.36
  342.0 4.1 copy-start.37
  343.6 2.6 copy-start.39
  351.9 2.7 copy-start.36
  355.5 4.1 copy-start.37
  360.4 13.3 %copy-start.10 = (f32[512,512]{1,0:T(8,128)S(1)}, f32[512,512]{1,0:T(8,128)}, u32[]{:S(2)}) copy-start(f32[512,512]{1,0:T(8,128)} %copy-done.8) | copy-start | bytes 3145732
  363.2 13.0 %copy-start.3 = (f32[512,512]{1,0:T(8,128)S(1)}, f32[512,512]{1,0:T(8,128)}, u32[]{:S(2)}) copy-start(f32[512,512]{1,0:T(8,128)} %copy-done.2) | copy-start | bytes 3145732
  363.2 13.0 %copy-start.59 = (f32[512]{0:T(512)S(1)}, f32[512]{0:T(512)}, u32[]{:S(2)}) copy-start(f32[512]{0:T(512)} %copy-done.58) | copy-start | bytes 6148
  363.2 13.0 %copy-start.61 = (f32[512]{0:T(512)S(1)}, f32[512]{0:T(512)}, u32[]{:S(2)}) copy-start(f32[512]{0:T(512)} %copy-done.60) | copy-start | bytes 6148
  363.2 13.0 %copy-start.63 = (f32[512]{0:T(512)S(1)}, f32[512]{0:T(512)}, u32[]{:S(2)}) copy-start(f32[512]{0:T(512)} %param.40) | copy-start | bytes 6148
  363.2 13.0 %copy-start.65 = (f32[512]{0:T(512)S(1)}, f32[512]{0:T(512)}, u32[]{:S(2)}) copy-start(f32[512]{0:T(512)} %param.41) | copy-start | bytes 6148
  368.2 41.1 %all-to-all-start.7 = ((bf16[2,1024,3,1,128]{4,0,3,2,1:T(2,128)(2,1)}), bf16[2,1024,3,1,128]{4,0,3,2,1:T(2,128)(2,1)}, u32[]{:S(2)}, u32[]{:S(2)}) async-start(bf16[2,1024,3,1,128]{4,0,3,2,1:T(2,128)(2,1)} %copy.216), calls=%async_computation.7 | async-start | bytes 3145728 | tf_op jit(solution)/shard_map/all_to_all | solution.py:310
  373.3 329.8 %all-reduce.4.cloned.1.call-start = ((), (), s32[]{:S(2)}) async-start(), calls=%async_computation.9 | async-start | bytes 33554432 | tf_op jit(solution)/shard_map/psum | solution.py:317
  376.2 5.2 copy-start.24
  376.2 5.2 copy-start.51
  381.4 3.5 copy-start.12
  381.4 3.5 copy-start.20
  381.4 4.9 copy-start.28
  381.4 4.9 copy-start.74
  386.4 4.6 copy-start.54
  393.1 23.1 %copy-start.49 = (bf16[2,256,512]{2,1,0:T(8,128)(2,1)S(1)}, bf16[2,256,512]{2,1,0:T(8,128)(2,1)}, u32[]{:S(2)}) copy-start(bf16[2,256,512]{2,1,0:T(8,128)(2,1)} %param.26) | copy-start | bytes 1572868
  703.1 3.7 copy-start.29
  706.8 6.5 copy-start.52
  708.6 5.7 copy-start.26
  714.2 3.7 copy-start.25
  714.2 5.7 copy-start.1
  (46 other events, 74.7 us)
Sparse Core Ops, SparseCore 0:
  419.0 284.0 all-reduce.3
